TPU v7x, 512 devices: a whole 4x4x16 slice. The times are simulated.
512 devices in a mesh: sx: 32 (over y, x, core), sy: 16 (over z).
Axes of the slice: x: 4, y: 4, z: 16, core: 2. Of those that a mesh axis runs over, the one named last changes fastest.
Arguments:
- inputs: bfloat16 [65536, 4096], P(('sx', 'sy')), may hold values from -6 to 6
- keys_in: bfloat16 [65536, 128], P(('sx', 'sy')), may hold values from -6 to 6
- queries: bfloat16 [65536, 128], P(('sx', 'sy')), may hold values from -6 to 6
- step_sizes: float32 [65536, 64], P(('sx', 'sy')), may hold values from 0.01 to 0.1
- level_weights: float32 [20, 64], replicated, may hold values from 0.3 to 3
- skip_gain: float32 [64], replicated, may hold values from 0.5 to 1.5
Outputs:
- outputs: bfloat16 [65536, 4096], P(('sx', 'sy'))
All inputs are finite; a program needn't handle non-finite values.
Results may differ from a plain program's by a relative error of at most 0.005.
Values sent between devices are 32-bit elements; how exact they have to be, the bound alone decides.
A program may use at most 64 MiB of HBM per device.

v0:
```python
import jax
import jax.numpy as jnp
from jax import lax
from jax.sharding import PartitionSpec as P

STRETCH = 64


def swapped(block, axis, distance):
    count = lax.axis_size(axis)
    route = []
    for low in range(count):
        high = low | 1 << distance
        if high != low and high < count:
            route += [(low, high), (high, low)]
    return lax.ppermute(block, axis, route)


def add_level(outputs, folded, queries_f32, partner, scale_vec):
    term = partner * scale_vec[None, :]
    return (outputs + jnp.dot(queries_f32, term, precision=lax.Precision.HIGHEST), folded)


def high_levels(
    my_columns, level_weights, index_low, index_high, head_share, head_dim, first_depth, bits_high
):
    high_sum = jnp.zeros_like(my_columns)
    for level_bit in range(bits_high):
        partner = swapped(my_columns, "sx", level_bit)
        upper_half = (index_high // 2**level_bit % 2).astype(jnp.float32)
        level_depth = first_depth + level_bit
        row_share = lax.dynamic_slice_in_dim(
            level_weights[level_depth + 1], index_low * head_share, head_share, 0
        )
        scale_vec = upper_half * jnp.repeat(
            row_share * (2.0**level_depth * STRETCH) ** (-0.5), head_dim
        )
        high_sum = high_sum + partner * scale_vec[None, :]
        my_columns = my_columns + partner
    return high_sum


def on_device(inputs, keys_in, queries, step_sizes, level_weights, skip_gain):
    tok_rows, full_width = inputs.shape
    num_heads = step_sizes.shape[1]
    head_dim = full_width // num_heads
    state_dim = keys_in.shape[1]
    block_count = tok_rows // STRETCH
    local_bits = block_count.bit_length() - 1
    highest = lax.Precision.HIGHEST
    values = (
        (inputs.astype(jnp.float32).reshape(tok_rows, num_heads, head_dim) * step_sizes[:, :, None])
        .reshape(tok_rows, full_width)
        .astype(jnp.bfloat16)
    )
    key_blocks = keys_in.reshape(block_count, STRETCH, state_dim)
    query_blocks = queries.reshape(block_count, STRETCH, state_dim)
    value_blocks = values.reshape(block_count, STRETCH, full_width)
    block_states = jnp.einsum(
        "bcn,bcw->bnw", key_blocks, value_blocks, preferred_element_type=jnp.float32
    )
    scores = jnp.einsum(
        "btn,bsn->bts", query_blocks, key_blocks, preferred_element_type=jnp.float32
    )
    causal = lax.broadcasted_iota(jnp.int32, (STRETCH, STRETCH), 0) >= lax.broadcasted_iota(
        jnp.int32, (STRETCH, STRETCH), 1
    )
    scores = jnp.where(causal[None], scores, 0.0) * STRETCH ** (-0.5)
    intra_weights = (scores[:, None] * level_weights[0][None, :, None, None]).astype(jnp.bfloat16)
    intra_out = jnp.einsum(
        "bhts,bshp->bthp",
        intra_weights,
        value_blocks.reshape(block_count, STRETCH, num_heads, head_dim),
        preferred_element_type=jnp.float32,
    ).reshape(tok_rows, full_width)
    outputs = inputs.astype(jnp.float32) * jnp.repeat(skip_gain, head_dim)[None, :] + intra_out
    queries_f32 = queries.astype(jnp.float32)
    level_bit = 0
    half_span = 2**level_bit
    groups = block_count // (2 * half_span)
    lower_sum = block_states.reshape(groups, 2, half_span, state_dim, full_width)[:, 0].sum(axis=1)
    scale_vec = jnp.repeat(level_weights[level_bit + 1] * (half_span * STRETCH) ** (-0.5), head_dim)
    upper_rows = queries_f32.reshape(groups, 2, half_span * STRETCH, state_dim)[:, 1]
    level_part = jnp.einsum(
        "gtn,gnw->gtw", upper_rows, lower_sum * scale_vec[None, None, :], precision=highest
    )
    outputs = outputs + jnp.stack([jnp.zeros_like(level_part), level_part], axis=1).reshape(
        tok_rows, full_width
    )
    size_low = lax.axis_size("sy")
    size_high = lax.axis_size("sx")
    bits_low = size_low.bit_length() - 1
    bits_high = size_high.bit_length() - 1
    index_low = lax.axis_index("sy")
    index_high = lax.axis_index("sx")
    head_share = num_heads // size_low
    share_width = head_share * head_dim
    group_sum = block_states.sum(axis=0)
    folded = jnp.zeros((state_dim, full_width), jnp.float32)
    for level_bit in range(bits_low):
        partner = swapped(group_sum, "sy", level_bit)
        upper_half = (index_low // 2**level_bit % 2).astype(jnp.float32)
        level_depth = local_bits + level_bit
        scale_vec = upper_half * jnp.repeat(
            level_weights[level_depth + 1] * (2.0**level_depth * STRETCH) ** (-0.5), head_dim
        )
        outputs, folded = add_level(outputs, folded, queries_f32, partner, scale_vec)
        group_sum = group_sum + partner
    my_columns = lax.dynamic_slice_in_dim(group_sum, index_low * share_width, share_width, 1)
    high_sum = high_levels(
        my_columns,
        level_weights,
        index_low,
        index_high,
        head_share,
        head_dim,
        local_bits + bits_low,
        bits_high,
    )
    outputs = outputs + jnp.dot(
        queries_f32,
        lax.all_gather(high_sum, "sy", axis=1, tiled=True),
        precision=lax.Precision.HIGHEST,
    )
    return outputs.astype(jnp.bfloat16)


def solution(mesh):
    placed = (
        P(("sx", "sy"), None),
        P(("sx", "sy"), None),
        P(("sx", "sy"), None),
        P(("sx", "sy"), None),
        P(),
        P(),
    )
    return jax.shard_map(
        on_device, mesh=mesh, in_specs=placed, out_specs=P(("sx", "sy"), None), check_vma=False
    )
```

profile of v0, /device:TPU:4, one launch (start us, length us, event | category | flops | bytes accessed | tf_op | source)
XLA Modules:
  0.0 711.0 jit_solution(6802354924683908111)
XLA Ops:
  9.0 3.0 bitcast_reduce_fusion
  12.0 3.8 collective-permute-start
  15.8 45.6 %collective-permute-done = f32[128,4096]{0,1:T(8,128)S(1)} collective-permute-done((f32[128,4096]{0,1:T(8,128)S(1)}, f32[128,4096]{0,1:T(8,128)S(1)}, u32[]{:S(2)}, u32[]{:S(2)}) %collective-permute-start) | collective-permute-done | bytes 2097184 | tf_op jit(solution)/shard_map/ppermute | solution.py:16
  63.0 5.2 collective-permute-start.1
  68.2 89.9 %collective-permute-done.1 = f32[128,4096]{0,1:T(8,128)S(1)} collective-permute-done((f32[128,4096]{0,1:T(8,128)S(1)}, f32[128,4096]{0,1:T(8,128)S(1)}, u32[]{:S(2)}, u32[]{:S(2)}) %collective-permute-start.1) | collective-permute-done | bytes 2097184 | tf_op jit(solution)/shard_map/ppermute | solution.py:16
  159.5 9.1 %collective-permute-start.2 = (f32[128,4096]{0,1:T(8,128)S(1)}, f32[128,4096]{0,1:T(8,128)S(1)}, u32[]{:S(2)}, u32[]{:S(2)}) collective-permute-start(f32[128,4096]{0,1:T(8,128)S(1)} %add.113), channel_id=1, source_target_pairs={{0,4},{4,0},{1,5},{5,1},{2,6},{6,2},{3,7},{7,3},{8,12},{12,8},{9,1... | collective-permute-start | bytes 6291464 | tf_op jit(solution)/shard_map/ppermute | solution.py:16
  168.6 223.9 %collective-permute-done.2 = f32[128,4096]{0,1:T(8,128)S(1)} collective-permute-done((f32[128,4096]{0,1:T(8,128)S(1)}, f32[128,4096]{0,1:T(8,128)S(1)}, u32[]{:S(2)}, u32[]{:S(2)}) %collective-permute-start.2) | collective-permute-done | bytes 2097184 | tf_op jit(solution)/shard_map/ppermute | solution.py:16
  394.4 103.3 %collective-permute-start.3 = (f32[128,4096]{0,1:T(8,128)}, f32[128,4096]{0,1:T(8,128)}, u32[]{:S(2)}, u32[]{:S(2)}) collective-permute-start(f32[128,4096]{0,1:T(8,128)} %add.116), channel_id=1, source_target_pairs={{0,8},{8,0},{1,9},{9,1},{2,10},{10,2},{3,11},{11,3},{4,12},{12,4},... | collective-permute-start | bytes 6291464 | tf_op jit(solution)/shard_map/ppermute | solution.py:16
  497.7 91.3 %collective-permute-done.3 = f32[128,4096]{0,1:T(8,128)} collective-permute-done((f32[128,4096]{0,1:T(8,128)}, f32[128,4096]{0,1:T(8,128)}, u32[]{:S(2)}, u32[]{:S(2)}) %collective-permute-start.3) | collective-permute-done | bytes 2097184 | tf_op jit(solution)/shard_map/ppermute | solution.py:16
  593.2 3.1 collective-permute-start.5
  596.3 4.3 collective-permute-done.5
  603.2 5.9 collective-permute-done.6
  609.1 3.5 collective-permute-start.7
  615.9 5.3 collective-permute-start.8
  628.1 2.9 convolution_bitcast_fusion.6
  631.0 5.8 copy.26
  636.8 5.4 reshape.209
  642.2 3.0 convolution_bitcast_fusion.5
  646.7 3.0 copy.24
  649.8 2.5 convolution_bitcast_fusion.3
  654.7 4.2 convolution_bitcast_fusion.1
  658.9 34.8 %all-gather.2.cloned.1.call-done = f32[128,4096]{0,1:T(8,128)} async-done(((f32[128,256]{0,1:T(8,128)}), f32[128,4096]{0,1:T(8,128)}) %all-gather.2.cloned.1.call-update) | async-done | bytes 2097168 | tf_op jit(solution)/shard_map/all_gather | solution.py:122
  693.7 2.8 convolution_bitcast_fusion
  696.5 5.3 fusion.5
  (73 shorter events, 30.3 us)
Async XLA Ops:
  6.5 2.4 copy-start
  6.5 1.6 copy-start.9
  6.5 687.2 %all-gather.2.cloned.1.call-start = ((), (), s32[]{:S(2)}) async-start(), calls=%async_computation | async-start | bytes 2228224 | tf_op jit(solution)/shard_map/all_gather | solution.py:122
  12.0 49.4 %collective-permute-start = (f32[128,4096]{0,1:T(8,128)S(1)}, f32[128,4096]{0,1:T(8,128)S(1)}, u32[]{:S(2)}, u32[]{:S(2)}) collective-permute-start(f32[128,4096]{0,1:T(8,128)S(1)} %get-tuple-element.16), channel_id=1, source_target_pairs={{0,1},{1,0},{2,3},{3,2},{4,5},{5,4},{6,7},{7,6},{8,9},{9,8},{10,11... | collective-permute-start | bytes 6291464 | tf_op jit(solution)/shard_map/ppermute | solution.py:16
  61.4 1.4 copy-start.5
  63.0 95.1 %collective-permute-start.1 = (f32[128,4096]{0,1:T(8,128)S(1)}, f32[128,4096]{0,1:T(8,128)S(1)}, u32[]{:S(2)}, u32[]{:S(2)}) collective-permute-start(f32[128,4096]{0,1:T(8,128)S(1)} %add.110), channel_id=1, source_target_pairs={{0,2},{2,0},{1,3},{3,1},{4,6},{6,4},{5,7},{7,5},{8,10},{10,8},{9,1... | collective-permute-start | bytes 6291464 | tf_op jit(solution)/shard_map/ppermute | solution.py:16
  158.1 1.3 copy-start.1
  159.5 233.0 %collective-permute-start.2 = (f32[128,4096]{0,1:T(8,128)S(1)}, f32[128,4096]{0,1:T(8,128)S(1)}, u32[]{:S(2)}, u32[]{:S(2)}) collective-permute-start(f32[128,4096]{0,1:T(8,128)S(1)} %add.113), channel_id=1, source_target_pairs={{0,4},{4,0},{1,5},{5,1},{2,6},{6,2},{3,7},{7,3},{8,12},{12,8},{9,1... | collective-permute-start | bytes 6291464 | tf_op jit(solution)/shard_map/ppermute | solution.py:16
  392.4 2.0 copy-start.3
  394.4 194.6 %collective-permute-start.3 = (f32[128,4096]{0,1:T(8,128)}, f32[128,4096]{0,1:T(8,128)}, u32[]{:S(2)}, u32[]{:S(2)}) collective-permute-start(f32[128,4096]{0,1:T(8,128)} %add.116), channel_id=1, source_target_pairs={{0,8},{8,0},{1,9},{9,1},{2,10},{10,2},{3,11},{11,3},{4,12},{12,4},... | collective-permute-start | bytes 6291464 | tf_op jit(solution)/shard_map/ppermute | solution.py:16
  589.9 3.2 collective-permute-start.4
  593.2 7.4 %collective-permute-start.5 = (f32[128,256]{0,1:T(8,128)S(1)}, f32[128,256]{0,1:T(8,128)S(1)}, u32[]{:S(2)}, u32[]{:S(2)}) collective-permute-start(f32[128,256]{0,1:T(8,128)S(1)} %add.123), channel_id=1, source_target_pairs={{0,32},{32,0},{16,48},{48,16},{64,96},{96,64},{80,112},{112,80},{1... | collective-permute-start | bytes 393224 | tf_op jit(solution)/shard_map/ppermute | solution.py:16
  600.7 8.4 %collective-permute-start.6 = (f32[128,256]{0,1:T(8,128)S(1)}, f32[128,256]{0,1:T(8,128)S(1)}, u32[]{:S(2)}, u32[]{:S(2)}) collective-permute-start(f32[128,256]{0,1:T(8,128)S(1)} %add.126), channel_id=1, source_target_pairs={{0,64},{64,0},{16,80},{80,16},{32,96},{96,32},{48,112},{112,48},{1... | collective-permute-start | bytes 393224 | tf_op jit(solution)/shard_map/ppermute | solution.py:16
  609.1 6.9 collective-permute-start.7
  615.9 8.4 %collective-permute-start.8 = (f32[128,256]{0,1:T(8,128)S(1)}, f32[128,256]{0,1:T(8,128)S(1)}, u32[]{:S(2)}, u32[]{:S(2)}) collective-permute-start(f32[128,256]{0,1:T(8,128)S(1)} %add.132), channel_id=1, source_target_pairs={{0,256},{256,0},{16,272},{272,16},{32,288},{288,32},{48,304},{304,... | collective-permute-start | bytes 393224 | tf_op jit(solution)/shard_map/ppermute | solution.py:16
  622.2 5.6 copy-start.10
  622.2 5.8 copy-start.8
  646.7 3.1 copy-start.2
  649.8 2.5 copy-start.4
  658.9 37.6 %copy-start.6 = (f32[128,4096]{0,1:T(8,128)S(1)}, f32[128,4096]{0,1:T(8,128)}, u32[]{:S(2)}) copy-start(f32[128,4096]{0,1:T(8,128)} %copy-done.5) | copy-start | bytes 6291460
  693.7 2.8 copy-start.7
Sparse Core Ops, SparseCore 0:
  625.3 68.3 all-gather.1
where the time goes:
time: 712 us; the launch traced here: 711 us
  waiting for transfers between devices  501 us (70%)
  starting transfers between devices  138 us (19%)
  local copies, waits for them, and re-layouts  26.5 us (4%)
  matrix products  26.3 us (4%)
  between operations  13.8 us (2%)
    ppermute x9, waiting for transfers between devices, swapped(): return lax.ppermute(block, axis, route)  467 us
    ppermute x9, starting transfers between devices, swapped(): return lax.ppermute(block, axis, route)  138 us
    all_gather x1, waiting for transfers between devices, on_device(): lax.all_gather(high_sum, 'sy', axis=1, tiled=True)  34.8 us
    dot_general x4, matrix products, add_level(): jnp.dot(queries_f32, term, precision=lax.Precision.HIGHEST)  14.4 us
  transfers between devices with their start and end apart: 10, of which 10 were waited for; matrix products, arithmetic and copies ran while one was open for 5% of the time, Pallas kernels for 0%

commit v1 on v0

--- a/solution.py
+++ b/solution.py
@@ -119,7 +119,9 @@
     )
     outputs = outputs + jnp.dot(
         queries_f32,
-        lax.all_gather(high_sum, "sy", axis=1, tiled=True),
+        jnp.concatenate(
+            lax.all_to_all(jnp.stack([high_sum] * lax.axis_size("sy")), "sy", 0, 0), axis=1
+        ),
         precision=lax.Precision.HIGHEST,
     )
     return outputs.astype(jnp.bfloat16)

time: 712 us -> 728 us (1.022)
  the two profiles are of different devices: /device:TPU:4 before, /device:TPU:36 now
where the time goes in v1:
time: 728 us
  waiting for transfers between devices  472 us (65%)
  starting transfers between devices  194 us (27%)
  local copies, waits for them, and re-layouts  28 us (4%)
  matrix products  27.9 us (4%)
    ppermute x9, waiting for transfers between devices, swapped(): return lax.ppermute(block, axis, route)  416 us
    all_to_all x1, starting transfers between devices, on_device(): lax.all_to_all(jnp.stack([high_sum] * lax.axis_size('sy')), 'sy', 0, 0)  149 us
    all_to_all x1, waiting for transfers between devices, on_device(): lax.all_to_all(jnp.stack([high_sum] * lax.axis_size('sy')), 'sy', 0, 0)  56.6 us
    ppermute x9, starting transfers between devices, swapped(): return lax.ppermute(block, axis, route)  45.5 us
    dot_general x4, matrix products, add_level(): jnp.dot(queries_f32, term, precision=lax.Precision.HIGHEST)  16 us
  transfers between devices with their start and end apart: 10, of which 10 were waited for; matrix products, arithmetic and copies ran while one was open for 5% of the time, Pallas kernels for 0%

profile of v1, /device:TPU:36, one launch (start us, length us, event | category | flops | bytes accessed | tf_op | source)
XLA Modules:
  0.0 727.7 jit_solution(7208010800379316985)
XLA Ops:
  2.4 3.0 bitcast_reduce_fusion
  7.5 47.2 %collective-permute-done = f32[128,4096]{0,1:T(8,128)S(1)} collective-permute-done((f32[128,4096]{0,1:T(8,128)S(1)}, f32[128,4096]{0,1:T(8,128)S(1)}, u32[]{:S(2)}, u32[]{:S(2)}) %collective-permute-start) | collective-permute-done | bytes 2097184 | tf_op jit(solution)/shard_map/ppermute | solution.py:16
  56.3 5.2 collective-permute-start.1
  61.5 88.9 %collective-permute-done.1 = f32[128,4096]{0,1:T(8,128)S(1)} collective-permute-done((f32[128,4096]{0,1:T(8,128)S(1)}, f32[128,4096]{0,1:T(8,128)S(1)}, u32[]{:S(2)}, u32[]{:S(2)}) %collective-permute-start.1) | collective-permute-done | bytes 2097184 | tf_op jit(solution)/shard_map/ppermute | solution.py:16
  151.7 9.1 %collective-permute-start.2 = (f32[128,4096]{0,1:T(8,128)S(1)}, f32[128,4096]{0,1:T(8,128)S(1)}, u32[]{:S(2)}, u32[]{:S(2)}) collective-permute-start(f32[128,4096]{0,1:T(8,128)S(1)} %add.113), channel_id=1, source_target_pairs={{0,4},{4,0},{1,5},{5,1},{2,6},{6,2},{3,7},{7,3},{8,12},{12,8},{9,1... | collective-permute-start | bytes 6291464 | tf_op jit(solution)/shard_map/ppermute | solution.py:16
  160.8 133.6 %collective-permute-done.2 = f32[128,4096]{0,1:T(8,128)S(1)} collective-permute-done((f32[128,4096]{0,1:T(8,128)S(1)}, f32[128,4096]{0,1:T(8,128)S(1)}, u32[]{:S(2)}, u32[]{:S(2)}) %collective-permute-start.2) | collective-permute-done | bytes 2097184 | tf_op jit(solution)/shard_map/ppermute | solution.py:16
  296.3 13.2 %collective-permute-start.3 = (f32[128,4096]{0,1:T(8,128)}, f32[128,4096]{0,1:T(8,128)}, u32[]{:S(2)}, u32[]{:S(2)}) collective-permute-start(f32[128,4096]{0,1:T(8,128)} %add.116), channel_id=1, source_target_pairs={{0,8},{8,0},{1,9},{9,1},{2,10},{10,2},{3,11},{11,3},{4,12},{12,4},... | collective-permute-start | bytes 6291464 | tf_op jit(solution)/shard_map/ppermute | solution.py:16
  309.5 129.9 %collective-permute-done.3 = f32[128,4096]{0,1:T(8,128)} collective-permute-done((f32[128,4096]{0,1:T(8,128)}, f32[128,4096]{0,1:T(8,128)}, u32[]{:S(2)}, u32[]{:S(2)}) %collective-permute-start.3) | collective-permute-done | bytes 2097184 | tf_op jit(solution)/shard_map/ppermute | solution.py:16
  443.7 3.1 collective-permute-start.5
  446.8 4.3 collective-permute-done.5
  453.6 5.9 collective-permute-done.6
  459.5 3.5 collective-permute-start.7
  466.4 5.1 collective-permute-start.8
  476.5 148.8 %all-to-all-start = ((f32[16,128,256]{1,2,0:T(8,128)}), f32[16,128,256]{1,2,0:T(8,128)}, u32[]{:S(2)}, u32[]{:S(2)}) async-start(f32[16,128,256]{1,2,0:T(8,128)} %stack.8), calls=%async_computation | async-start | bytes 4194304 | tf_op jit(solution)/shard_map/all_to_all | solution.py:123
  628.2 2.9 convolution_bitcast_fusion.6
  631.1 5.8 copy.19
  637.0 5.4 reshape.219
  642.4 3.0 convolution_bitcast_fusion.5
  646.9 3.0 copy.17
  649.9 2.5 convolution_bitcast_fusion.3
  654.9 4.4 convolution_bitcast_fusion.1
  659.2 56.6 %all-to-all-done = f32[16,128,256]{1,2,0:T(8,128)} async-done(((f32[16,128,256]{1,2,0:T(8,128)}), f32[16,128,256]{1,2,0:T(8,128)}, u32[]{:S(2)}, u32[]{:S(2)}) %all-to-all-start) | async-done | bytes 2097184 | tf_op jit(solution)/shard_map/all_to_all | solution.py:123
  715.8 2.8 convolution_bitcast_fusion
  718.7 6.8 fusion.5
  (75 shorter events, 33.3 us)
Async XLA Ops:
  0.0 2.4 copy-start
  0.0 1.6 copy-start.10
  5.5 49.3 %collective-permute-start = (f32[128,4096]{0,1:T(8,128)S(1)}, f32[128,4096]{0,1:T(8,128)S(1)}, u32[]{:S(2)}, u32[]{:S(2)}) collective-permute-start(f32[128,4096]{0,1:T(8,128)S(1)} %get-tuple-element.16), channel_id=1, source_target_pairs={{0,1},{1,0},{2,3},{3,2},{4,5},{5,4},{6,7},{7,6},{8,9},{9,8},{10,11... | collective-permute-start | bytes 6291464 | tf_op jit(solution)/shard_map/ppermute | solution.py:16
  54.7 1.4 copy-start.5
  56.3 94.1 %collective-permute-start.1 = (f32[128,4096]{0,1:T(8,128)S(1)}, f32[128,4096]{0,1:T(8,128)S(1)}, u32[]{:S(2)}, u32[]{:S(2)}) collective-permute-start(f32[128,4096]{0,1:T(8,128)S(1)} %add.110), channel_id=1, source_target_pairs={{0,2},{2,0},{1,3},{3,1},{4,6},{6,4},{5,7},{7,5},{8,10},{10,8},{9,1... | collective-permute-start | bytes 6291464 | tf_op jit(solution)/shard_map/ppermute | solution.py:16
  150.4 1.3 copy-start.1
  151.7 142.7 %collective-permute-start.2 = (f32[128,4096]{0,1:T(8,128)S(1)}, f32[128,4096]{0,1:T(8,128)S(1)}, u32[]{:S(2)}, u32[]{:S(2)}) collective-permute-start(f32[128,4096]{0,1:T(8,128)S(1)} %add.113), channel_id=1, source_target_pairs={{0,4},{4,0},{1,5},{5,1},{2,6},{6,2},{3,7},{7,3},{8,12},{12,8},{9,1... | collective-permute-start | bytes 6291464 | tf_op jit(solution)/shard_map/ppermute | solution.py:16
  294.4 1.9 copy-start.3
  296.3 143.1 %collective-permute-start.3 = (f32[128,4096]{0,1:T(8,128)}, f32[128,4096]{0,1:T(8,128)}, u32[]{:S(2)}, u32[]{:S(2)}) collective-permute-start(f32[128,4096]{0,1:T(8,128)} %add.116), channel_id=1, source_target_pairs={{0,8},{8,0},{1,9},{9,1},{2,10},{10,2},{3,11},{11,3},{4,12},{12,4},... | collective-permute-start | bytes 6291464 | tf_op jit(solution)/shard_map/ppermute | solution.py:16
  440.4 3.2 collective-permute-start.4
  443.7 7.4 %collective-permute-start.5 = (f32[128,256]{0,1:T(8,128)S(1)}, f32[128,256]{0,1:T(8,128)S(1)}, u32[]{:S(2)}, u32[]{:S(2)}) collective-permute-start(f32[128,256]{0,1:T(8,128)S(1)} %add.123), channel_id=1, source_target_pairs={{0,32},{32,0},{16,48},{48,16},{64,96},{96,64},{80,112},{112,80},{1... | collective-permute-start | bytes 393224 | tf_op jit(solution)/shard_map/ppermute | solution.py:16
  451.1 8.4 %collective-permute-start.6 = (f32[128,256]{0,1:T(8,128)S(1)}, f32[128,256]{0,1:T(8,128)S(1)}, u32[]{:S(2)}, u32[]{:S(2)}) collective-permute-start(f32[128,256]{0,1:T(8,128)S(1)} %add.126), channel_id=1, source_target_pairs={{0,64},{64,0},{16,80},{80,16},{32,96},{96,32},{48,112},{112,48},{1... | collective-permute-start | bytes 393224 | tf_op jit(solution)/shard_map/ppermute | solution.py:16
  459.5 6.9 collective-permute-start.7
  466.4 8.4 %collective-permute-start.8 = (f32[128,256]{0,1:T(8,128)S(1)}, f32[128,256]{0,1:T(8,128)S(1)}, u32[]{:S(2)}, u32[]{:S(2)}) collective-permute-start(f32[128,256]{0,1:T(8,128)S(1)} %add.132), channel_id=1, source_target_pairs={{0,256},{256,0},{16,272},{272,16},{32,288},{288,32},{48,304},{304,... | collective-permute-start | bytes 393224 | tf_op jit(solution)/shard_map/ppermute | solution.py:16
  476.5 239.3 %all-to-all-start = ((f32[16,128,256]{1,2,0:T(8,128)}), f32[16,128,256]{1,2,0:T(8,128)}, u32[]{:S(2)}, u32[]{:S(2)}) async-start(f32[16,128,256]{1,2,0:T(8,128)} %stack.8), calls=%async_computation | async-start | bytes 4194304 | tf_op jit(solution)/shard_map/all_to_all | solution.py:123
  625.3 2.6 copy-start.11
  625.3 2.8 copy-start.9
  646.9 3.0 copy-start.2
  649.9 2.5 copy-start.4
  654.9 63.8 %copy-start.8 = (f32[128,4096]{0,1:T(8,128)S(1)}, f32[128,4096]{0,1:T(8,128)}, u32[]{:S(2)}) copy-start(f32[128,4096]{0,1:T(8,128)} %copy.17) | copy-start | bytes 6291460
  715.8 2.8 copy-start.6
  715.8 2.9 copy-start.7
